TPU v7x, 32 devices: a whole 2x2x4 slice. The times are simulated.
32 devices in a mesh: groups: 2 (over y), row: 4 (over z), col: 4 (over x, core).
Axes of the slice: x: 2, y: 2, z: 4, core: 2. Of those that a mesh axis runs over, the one named last changes fastest.
Arguments:
- descriptors: float32 [32, 8192], P(None, ('groups', 'row', 'col')), parts along dimension 1, may hold values from -6 to 6
- lengthscale: float32 [64], P('groups'), parts along dimension 0, may hold values from 1.8 to 3.6
- noise: float32 [32], P('groups'), parts along dimension 0, may hold values from 0.1 to 1
- direction: float32 [16, 8192], P(None, ('groups', 'row', 'col')), parts along dimension 1, may hold values from -22 to 22
- residual: float32 [16, 8192], P(None, ('groups', 'row', 'col')), parts along dimension 1, may hold values from -22 to 22
- solution: float32 [16, 8192], P(None, ('groups', 'row', 'col')), parts along dimension 1, may hold values from -6 to 6
Outputs:
- new_solution: float32 [16, 8192], P(None, ('groups', 'row', 'col')), parts along dimension 1
- new_residual: float32 [16, 8192], P(None, ('groups', 'row', 'col')), parts along dimension 1
There are 2 independent parts, one for each index of `groups`. A program takes and returns all parts, laid end to end along the dimension named above; each array names one. Nothing has to cross between parts.
All inputs are finite; a program needn't handle non-finite values.
Results may differ from a plain program's by a relative error of at most 0.000076.
Values sent between devices are 32-bit elements; how exact they have to be, the bound alone decides.
A program may use at most 64 MiB of HBM per device.

v0:
```python
import jax
import jax.numpy as jnp
import numpy as np
from jax import lax
from jax.sharding import PartitionSpec as P

highest = lax.Precision.HIGHEST


def rule_index(first_block, second_block, coord_sum):
    return first_block <= second_block


def pair_tables(rows_total, cols_total, pick_rule):
    listed = {}
    longest = 1
    for grid_row in range(rows_total):
        for grid_col in range(cols_total):
            for block_col in range(cols_total):
                first_block = grid_row * cols_total + block_col
                picks = []
                for other_row in range(rows_total):
                    second_block = other_row * cols_total + grid_col
                    coord_sum = grid_row + other_row + block_col + grid_col
                    if pick_rule(first_block, second_block, coord_sum):
                        picks.append((other_row, 1.0 if first_block != second_block else 0.0))
                listed[grid_row, grid_col, block_col] = picks
                longest = max(longest, len(picks))
    table_rows = np.zeros((rows_total, cols_total, cols_total, longest), np.int32)
    table_keep = np.zeros((rows_total, cols_total, cols_total, longest), np.float32)
    table_mirror = np.zeros((rows_total, cols_total, cols_total, longest), np.float32)
    for place_key, picks in listed.items():
        for slot, entry in enumerate(picks):
            table_rows[place_key + (slot,)] = entry[0]
            table_keep[place_key + (slot,)] = 1.0
            table_mirror[place_key + (slot,)] = entry[1]
    return (table_rows, table_keep, table_mirror)


def shards(descriptors, lengthscale, noise, direction, residual, solution):
    points = descriptors.shape[1]
    width = direction.shape[0]
    depth = descriptors.shape[0]
    rows_total = lax.axis_size("row")
    cols_total = lax.axis_size("col")
    my_row = lax.axis_index("row")
    my_col = lax.axis_index("col")
    scaled = descriptors / lengthscale[:, None]
    column_x, column_p = (
        lax.all_gather(scaled, "row", axis=1, tiled=True),
        lax.all_gather(direction, "row", axis=1, tiled=True),
    )
    column_sq = jnp.sum(column_x * column_x, axis=0).reshape(rows_total, points)
    column_x3 = column_x.reshape(depth, rows_total, points)
    column_p3 = column_p.reshape(width, rows_total, points)
    table_rows, table_keep, table_mirror = pair_tables(rows_total, cols_total, rule_index)
    dev_rows = jnp.asarray(table_rows)[my_row, my_col]
    dev_keep = jnp.asarray(table_keep)[my_row, my_col]
    dev_mirror = jnp.asarray(table_mirror)[my_row, my_col]
    row_labels = jnp.arange(rows_total, dtype=jnp.int32)
    start_row = jnp.zeros((width, cols_total * points), jnp.float32)
    start_col = jnp.zeros((width, rows_total * points), jnp.float32)
    offset = jnp.int32(0)
    piece_x = lax.all_gather(scaled, "col", axis=1, tiled=True)
    piece_p = lax.all_gather(direction, "col", axis=1, tiled=True)
    blocks = piece_x.shape[1] // points

    def per_block(which, state):
        row_acc, col_acc = state
        left_x = lax.dynamic_slice_in_dim(piece_x, which * points, points, 1)
        left_p = lax.dynamic_slice_in_dim(piece_p, which * points, points, 1)
        left_sq = jnp.sum(left_x * left_x, axis=0)
        block_col = offset // points + which
        picked = lax.dynamic_index_in_dim(dev_rows, block_col, 0, keepdims=False)
        keep = lax.dynamic_index_in_dim(dev_keep, block_col, 0, keepdims=False)
        right_x = jnp.take(column_x3, picked, axis=1)
        right_p = jnp.take(column_p3, picked, axis=1)
        right_sq = jnp.take(column_sq, picked, axis=0)
        cross = jnp.einsum("di,dmj->mij", left_x, right_x, precision=highest)
        kernel = jnp.exp(-0.5 * (left_sq[None, :, None] + right_sq[:, None, :] - 2.0 * cross))
        kernel = kernel * keep[:, None, None]
        row_add = jnp.einsum("hmj,mij->hi", right_p, kernel, precision=highest)
        place = block_col * points
        current = lax.dynamic_slice_in_dim(row_acc, place, points, 1)
        row_acc = lax.dynamic_update_slice_in_dim(row_acc, current + row_add, place, 1)
        mirror_w = lax.dynamic_index_in_dim(dev_mirror, block_col, 0, keepdims=False)
        onehot = (picked[:, None] == row_labels[None, :]).astype(jnp.float32) * mirror_w[:, None]
        weighted = jnp.einsum("mij,mr->rij", kernel, onehot, precision=highest)
        col_add = jnp.einsum("hi,rij->hrj", left_p, weighted, precision=highest)
        col_acc = col_acc + col_add.reshape(width, rows_total * points)
        return (row_acc, col_acc)

    row_acc, col_acc = lax.fori_loop(0, blocks, per_block, (start_row, start_col))
    product = lax.psum_scatter(row_acc, "col", scatter_dimension=1, tiled=True)
    product = product + lax.psum_scatter(col_acc, "row", scatter_dimension=1, tiled=True)
    image = product + noise[:, None] * direction
    local_sq = jnp.sum(residual * residual, axis=1)
    local_curve = jnp.sum(direction * image, axis=1)
    resid_sq, curvature = lax.psum((local_sq, local_curve), ("row", "col"))
    alpha = resid_sq / curvature
    return (solution + alpha[:, None] * direction, residual - alpha[:, None] * image)


def solution(mesh):
    in_specs = (
        P(None, ("groups", "row", "col")),
        P("groups"),
        P("groups"),
        P(None, ("groups", "row", "col")),
        P(None, ("groups", "row", "col")),
        P(None, ("groups", "row", "col")),
    )
    out_specs = (P(None, ("groups", "row", "col")), P(None, ("groups", "row", "col")))
    return jax.shard_map(shards, mesh=mesh, in_specs=in_specs, out_specs=out_specs, check_vma=False)
```

profile of v0, /device:TPU:0, one launch (start us, length us, event | category | flops | bytes accessed | tf_op | source)
XLA Modules:
  0.0 157.5 jit_solution(4909193700356809203)
XLA Ops:
  7.2 0.7 copy-done.2
  7.9 6.2 %all_gather.15 = f32[16,1024]{1,0:T(8,128)S(1)} all-gather(f32[16,256]{1,0:T(8,128)S(1)} %copy-done.2), channel_id=1, replica_groups=mesh['groups'=2,'row'=4,'col'=4] {'col'}, dimensions={1}, use_global_device_ids=true | all-gather | bytes 81920 | tf_op jit(solution)/shard_map/all_gather | solution.py:65
  14.1 14.0 %all_gather.12 = f32[16,1024]{1,0:T(8,128)S(1)} all-gather(f32[16,256]{1,0:T(8,128)S(1)} %copy-done.2), channel_id=1, replica_groups=mesh['groups'=2,'row'=4,'col'=4] {'row'}, dimensions={1}, use_global_device_ids=true | all-gather | bytes 81920 | tf_op jit(solution)/shard_map/all_gather | solution.py:51
  28.0 0.7 copy-done.9
  28.8 13.4 %all_gather.14 = f32[32,1024]{1,0:T(8,128)S(1)} all-gather(f32[32,256]{1,0:T(8,128)S(1)} %broadcast_divide_fusion), channel_id=1, replica_groups=mesh['groups'=2,'row'=4,'col'=4] {'row'}, dimensions={1}, use_global_device_ids=true | all-gather | bytes 163840 | tf_op jit(solution)/shard_map/all_gather | solution.py:50
  42.2 5.4 %all_gather.13 = f32[32,1024]{1,0:T(8,128)S(1)} all-gather(f32[32,256]{1,0:T(8,128)S(1)} %broadcast_divide_fusion), channel_id=1, replica_groups=mesh['groups'=2,'row'=4,'col'=4] {'col'}, dimensions={1}, use_global_device_ids=true | all-gather | bytes 163840 | tf_op jit(solution)/shard_map/all_gather | solution.py:64
  47.7 0.7 dynamic-slice_bitcast_fusion.2
  48.4 0.7 dynamic-slice_bitcast_fusion
  49.1 27.1 %while.18 = (s32[]{:T(128)}, f32[16,1024]{1,0:T(8,128)S(1)}, f32[16,1024]{1,0:T(8,128)S(1)}, s32[4,4]{1,0:T(4,128)S(1)}, f32[16,4,256]{2,0,1:T(8,128)S(1)}, /*in...) while((s32[]{:T(128)}, f32[16,1024]{1,0:T(8,128)S(1)}, ...), condition=%wide.region_5.6_spmd.clone, body=%wide.region_3.5_spmd.clone.sunk | while | flops 215324480 | bytes 8466385 | solution.py:93
  49.2 0.6 gather_fusion
  49.8 0.6 gather_fusion.2
  50.4 0.6 gather_fusion.1
  50.9 1.3 fusion.63
  52.3 0.6 fusion.64
  52.9 0.4 copy.36
  53.3 1.8 %fusion.65 = f32[4,256,256]{2,0,1:T(4,128)S(1)} fusion(f32[4,256,256]{2,0,1:T(4,128)S(1)} %copy.36, f32[4]{0:T(128)S(1)} %get-tuple-element.445, s32[4]{0:T(128)S(1)} %get-tuple-element.446), kind=kOutput, calls=%fused_computation.32.clone.1 | convolution fusion | flops 12582944 | bytes 2097184 | tf_op jit(solution)/shard_map/while/body/eval_jaxpr/mij,mr->rij/dot_general | solution.py:88
  55.1 0.7 convolution_bitcast_fusion.3
  56.0 0.6 gather_fusion
  56.6 0.6 gather_fusion.2
  57.2 0.6 gather_fusion.1
  57.7 1.3 fusion.63
  59.0 0.6 fusion.64
  59.6 0.4 copy.36
  60.0 1.8 %fusion.65 = f32[4,256,256]{2,0,1:T(4,128)S(1)} fusion(f32[4,256,256]{2,0,1:T(4,128)S(1)} %copy.36, f32[4]{0:T(128)S(1)} %get-tuple-element.445, s32[4]{0:T(128)S(1)} %get-tuple-element.446), kind=kOutput, calls=%fused_computation.32.clone.1 | convolution fusion | flops 12582944 | bytes 2097184 | tf_op jit(solution)/shard_map/while/body/eval_jaxpr/mij,mr->rij/dot_general | solution.py:88
  61.8 0.7 convolution_bitcast_fusion.3
  62.7 0.6 gather_fusion
  63.4 0.6 gather_fusion.2
  63.9 0.6 gather_fusion.1
  64.5 1.3 fusion.63
  65.8 0.6 fusion.64
  66.4 0.4 copy.36
  66.8 1.8 %fusion.65 = f32[4,256,256]{2,0,1:T(4,128)S(1)} fusion(f32[4,256,256]{2,0,1:T(4,128)S(1)} %copy.36, f32[4]{0:T(128)S(1)} %get-tuple-element.445, s32[4]{0:T(128)S(1)} %get-tuple-element.446), kind=kOutput, calls=%fused_computation.32.clone.1 | convolution fusion | flops 12582944 | bytes 2097184 | tf_op jit(solution)/shard_map/while/body/eval_jaxpr/mij,mr->rij/dot_general | solution.py:88
  68.6 0.7 convolution_bitcast_fusion.3
  69.5 0.6 gather_fusion
  70.1 0.6 gather_fusion.2
  70.7 0.6 gather_fusion.1
  71.3 1.3 fusion.63
  72.6 0.6 fusion.64
  73.2 0.4 copy.36
  73.6 1.8 %fusion.65 = f32[4,256,256]{2,0,1:T(4,128)S(1)} fusion(f32[4,256,256]{2,0,1:T(4,128)S(1)} %copy.36, f32[4]{0:T(128)S(1)} %get-tuple-element.445, s32[4]{0:T(128)S(1)} %get-tuple-element.446), kind=kOutput, calls=%fused_computation.32.clone.1 | convolution fusion | flops 12582944 | bytes 2097184 | tf_op jit(solution)/shard_map/while/body/eval_jaxpr/mij,mr->rij/dot_general | solution.py:88
  75.4 0.7 convolution_bitcast_fusion.3
  76.2 0.6 copy-done
  76.9 0.7 reduce-scatter.3.cloned.1.call-update
  77.7 19.3 %reduce-scatter.5.cloned.1.call-done = f32[16,256]{1,0:T(8,128)} async-done(((f32[16,1024]{1,0:T(8,128)}), f32[16,256]{1,0:T(8,128)}) %reduce-scatter.5.cloned.1.call-update) | async-done | bytes 16400 | tf_op jit(solution)/shard_map/reduce_scatter | solution.py:95
  97.0 20.2 %reduce-scatter.3.cloned.1.call-done = f32[16,256]{1,0:T(8,128)} async-done(((f32[16,1024]{1,0:T(8,128)}), f32[16,256]{1,0:T(8,128)}) %reduce-scatter.3.cloned.1.call-update) | async-done | bytes 16400 | tf_op jit(solution)/shard_map/reduce_scatter | solution.py:94
  117.2 1.0 multiply_reduce_fusion.2
  118.2 31.8 %all-reduce = (f32[16]{0:T(128)S(1)}, f32[16]{0:T(128)S(1)}) all-reduce(f32[16]{0:T(128)S(1)} %multiply_reduce_fusion.3, f32[16]{0:T(128)S(1)} %multiply_reduce_fusion.2), channel_id=1, replica_groups=mesh['groups'=2,'row'=4,'col'=4] {'row','col'}, use_global_device_ids=true, to_apply=%region_1.2 | all-reduce | flops 32 | bytes 256 | tf_op jit(solution)/shard_map/psum | solution.py:99
  149.9 0.7 multiply_subtract_fusion
  (61 shorter events, 1.1 us)
Async XLA Ops:
  7.2 0.7 copy-start.2
  7.2 89.8 %reduce-scatter.5.cloned.1.call-start = ((), (), s32[]{:S(2)}) async-start(), calls=%async_computation.3 | async-start | bytes 81920 | tf_op jit(solution)/shard_map/reduce_scatter | solution.py:95
  14.1 14.0 %copy-start.6 = (f32[32,256]{1,0:T(8,128)S(1)}, f32[32,256]{1,0:T(8,128)}, u32[]{:S(2)}) copy-start(f32[32,256]{1,0:T(8,128)} %param.11) | copy-start | bytes 98308
  28.0 0.7 copy-start.9
  76.2 0.6 copy-start
  76.2 0.7 copy-start.1
  76.8 40.4 %reduce-scatter.3.cloned.1.call-start = ((), (), s32[]{:S(2)}) async-start(), calls=%async_computation.2 | async-start | bytes 81920 | tf_op jit(solution)/shard_map/reduce_scatter | solution.py:94
  76.9 0.7 copy-start.5
  77.6 39.6 %copy-start.8 = (f32[16]{0:T(128)S(1)}, f32[16]{0:T(128)}, u32[]{:S(2)}) copy-start(f32[16]{0:T(128)} %param.13) | copy-start | bytes 196
  117.2 32.7 %copy-start.3 = (f32[16,256]{1,0:T(8,128)S(1)}, f32[16,256]{1,0:T(8,128)}, u32[]{:S(2)}) copy-start(f32[16,256]{1,0:T(8,128)} %reduce-scatter.5.cloned.1.call-done) | copy-start | bytes 49156
  117.2 32.7 %copy-start.4 = (f32[16,256]{1,0:T(8,128)S(1)}, f32[16,256]{1,0:T(8,128)}, u32[]{:S(2)}) copy-start(f32[16,256]{1,0:T(8,128)} %reduce-scatter.3.cloned.1.call-done) | copy-start | bytes 49156
  117.2 32.7 %copy-start.7 = (f32[16,256]{1,0:T(8,128)S(1)}, f32[16,256]{1,0:T(8,128)}, u32[]{:S(2)}) copy-start(f32[16,256]{1,0:T(8,128)} %param.16) | copy-start | bytes 49156
Sparse Core Ops, SparseCore 0:
  76.9 19.9 reduce-scatter.4
  99.5 17.6 reduce-scatter.2
where the time goes:
time: 158 us; the launch traced here: 157 us
  blocking collectives  70.8 us (45%)
  waiting for transfers between devices  40.2 us (25%)
  matrix products  17.7 us (11%)
  between operations  14.1 us (9%)
  local copies, waits for them, and re-layouts  11.7 us (7%)
  other arithmetic  2.49 us (2%)
    psum x1, blocking collectives, shards(): resid_sq, curvature = lax.psum((local_sq, local_curve), ('row', 'col'))  31.8 us
    reduce_scatter x1, waiting for transfers between devices, shards(): product = lax.psum_scatter(row_acc, 'col', scatter_dimension=1, tiled=True)  20.2 us
    reduce_scatter x1, waiting for transfers between devices, shards(): lax.psum_scatter(col_acc, 'row', scatter_dimension=1, tiled=True)  19.3 us
    all_gather x1, blocking collectives, shards(): lax.all_gather(direction, 'row', axis=1, tiled=True)  14 us
    all_gather x1, blocking collectives, shards(): lax.all_gather(scaled, 'row', axis=1, tiled=True)  13.4 us
    dot_general x4, matrix products, per_block(): weighted = jnp.einsum('mij,mr->rij', kernel, onehot, precision=highest)  7.22 us
    all_gather x1, blocking collectives, shards(): piece_p = lax.all_gather(direction, 'col', axis=1, tiled=True)  6.17 us
    all_gather x1, blocking collectives, shards(): piece_x = lax.all_gather(scaled, 'col', axis=1, tiled=True)  5.41 us
  transfers between devices with their start and end apart: 2, of which 2 were waited for; matrix products, arithmetic and copies ran while one was open for 0% of the time, Pallas kernels for 0%

commit v1 on v0

v1 whole, which is shorter than its diff:
```python
import functools
import math

import jax
import jax.numpy as jnp
from jax import lax
from jax.experimental import pallas as pl
from jax.experimental.pallas import tpu as pltpu
from jax.sharding import PartitionSpec as P

MESH = pl.DeviceIdType.MESH
LOG2E = math.log2(math.e)
f32 = jnp.float32
bf16 = jnp.bfloat16


def split3(v):
    h = v.astype(bf16)
    rest = v - h.astype(f32)
    m = rest.astype(bf16)
    low = (rest - m.astype(f32)).astype(bf16)
    return h, m, low


def to_column(row, height):
    n = row.shape[1]
    wide = jnp.broadcast_to(row, (height, n))
    r = lax.broadcasted_iota(jnp.int32, (height, n), 0)
    c = lax.broadcasted_iota(jnp.int32, (height, n), 1)
    return jnp.sum(jnp.where(r == c, wide, 0.0), axis=1, keepdims=True)


def to_row(column, offset):
    h = column.shape[0]
    r = lax.broadcasted_iota(jnp.int32, (h, 128), 0)
    c = lax.broadcasted_iota(jnp.int32, (h, 128), 1)
    wide = jnp.broadcast_to(column, (h, 128))
    return jnp.sum(jnp.where(r + offset == c, wide, 0.0), axis=0, keepdims=True)


def half_square(x, xs):
    return -0.5 * jnp.sum(x * xs, axis=0, keepdims=True)


def square_rows(q, first):
    h, m, low = split3(q)
    n = q.shape[1]
    r = lax.broadcasted_iota(jnp.int32, (16, n), 0)
    base = 0 if first else 3
    other = (r >= 3 - base) & (r < 6 - base)
    out = jnp.where(other, 1.0, 0.0)
    for k, part in enumerate((h, m, low)):
        out = jnp.where(r == base + k, jnp.broadcast_to(part.astype(f32), (16, n)), out)
    return out.astype(bf16)


def stack_i(x):
    xs = x * LOG2E
    h, m, low = split3(xs)
    q = half_square(x, xs)
    pad = jnp.zeros((48, x.shape[1]), bf16)
    return jnp.concatenate([h, h, m, h, m, low, square_rows(q, True), pad], axis=0)


def stack_j(x):
    h, m, low = split3(x)
    q = half_square(x, x * LOG2E)
    pad = jnp.zeros((48, x.shape[1]), bf16)
    return jnp.concatenate([h, m, h, low, m, h, square_rows(q, False), pad], axis=0)


def kernel(R, C, x_ref, l_ref, n_ref, p_ref, r_ref, s_ref, sol_ref, res_ref,
           jbuf, ibuf, ist, part, rsbuf, stat,
           jsend, jrecv, isend, irecv, psend, precv, ssend, srecv):
    D, n = x_ref.shape
    H = p_ref.shape[0]
    my_row = lax.axis_index("row")
    my_col = lax.axis_index("col")

    def peer(dr, dc):
        return {"row": lax.rem(my_row + dr, R), "col": lax.rem(my_col + dc, C)}

    others = [(dr, dc) for dr in range(R) for dc in range(C) if dr or dc]
    barrier = pltpu.get_barrier_semaphore()
    for dr, dc in others:
        pl.semaphore_signal(barrier, inc=1, device_id=peer(dr, dc), device_id_type=MESH)

    jbuf[0, :D] = x_ref[...] / to_column(l_ref[...], D)
    jbuf[0, D:] = p_ref[...]
    noise = to_column(n_ref[...], H)

    pl.semaphore_wait(barrier, len(others))

    copies = []

    def remote(src, dst, send, recv, device):
        copy = pltpu.make_async_remote_copy(
            src_ref=src, dst_ref=dst, send_sem=send, recv_sem=recv,
            device_id=device, device_id_type=MESH)
        copy.start()
        copies.append(copy)
        return copy

    jcopy, icopy, pcopy, scopy = {}, {}, {}, {}
    for d in range(1, C):
        icopy[C - d] = remote(jbuf.at[0], ibuf.at[C - d], isend.at[C - d], irecv.at[C - d], peer(0, d))
    for d in range(1, R):
        jcopy[R - d] = remote(jbuf.at[0], jbuf.at[R - d], jsend.at[R - d], jrecv.at[R - d], peer(d, 0))

    resid = r_ref[...]
    resid_row = to_row(jnp.sum(resid * resid, axis=1, keepdims=True), H)
    mine = p_ref[...]
    curve = noise * mine * mine

    for jo in range(R):
        if jo:
            jcopy[jo].wait_recv()
        left = stack_j(jbuf[jo, :D])
        weights = jnp.concatenate(split3(jbuf[jo, D:]), axis=0)
        for s in range(C):
            if jo == 0:
                if s:
                    icopy[s].wait_recv()
                    ist[s] = stack_i(ibuf[s, :D])
                else:
                    ist[s] = stack_i(jbuf[0, :D])
            expo = lax.dot_general(left, ist[s], (((0,), (0,)), ((), ())), preferred_element_type=f32)
            k = jnp.exp2(expo)
            k1 = k.astype(bf16)
            k2 = (k - k1.astype(f32)).astype(bf16)
            got = jnp.dot(weights, k1, preferred_element_type=f32) + jnp.dot(weights, k2, preferred_element_type=f32)
            got = got[:H] + (got[H:2 * H] + got[2 * H:])
            if jo:
                got = part[s] + got
            part[s] = got
            if jo == R - 1:
                direction = ibuf[s, D:] if s else mine
                curve = curve + direction * got
                if s:
                    pcopy[C - s] = remote(part.at[s], rsbuf.at[C - s], psend.at[C - s], precv.at[C - s], peer(0, s))

    stat[0] = to_row(jnp.sum(curve, axis=1, keepdims=True), 0) + resid_row
    for dr, dc in others:
        slot = ((R - dr) % R) * C + (C - dc) % C
        scopy[slot] = remote(stat.at[0], stat.at[slot], ssend.at[slot], srecv.at[slot], peer(dr, dc))

    image = part[0] + noise * mine
    for s in range(1, C):
        pcopy[s].wait_recv()
        image = image + rsbuf[s]
    total = stat[0]
    for slot in range(1, R * C):
        scopy[slot].wait_recv()
        total = total + stat[slot]
    curvature = to_column(total, H)
    lane = lax.broadcasted_iota(jnp.int32, (H, 128), 1)
    sub = lax.broadcasted_iota(jnp.int32, (H, 128), 0)
    resid_sq = jnp.sum(jnp.where(lane == sub + H, jnp.broadcast_to(total, (H, 128)), 0.0), axis=1, keepdims=True)
    alpha = resid_sq / curvature
    sol_ref[...] = s_ref[...] + alpha * mine
    res_ref[...] = resid - alpha * image
    for copy in copies:
        copy.wait_send()


def shards(R, C, descriptors, lengthscale, noise, direction, residual, solution):
    D, n = descriptors.shape
    H = direction.shape[0]
    vmem = pl.BlockSpec(memory_space=pltpu.VMEM)
    dma = pltpu.SemaphoreType.DMA
    return pl.pallas_call(
        functools.partial(kernel, R, C),
        out_shape=(jax.ShapeDtypeStruct((H, n), f32), jax.ShapeDtypeStruct((H, n), f32)),
        in_specs=[vmem] * 6,
        out_specs=(vmem, vmem),
        scratch_shapes=[
            pltpu.VMEM((R, D + H, n), f32),
            pltpu.VMEM((C, D + H, n), f32),
            pltpu.VMEM((C, 256, n), bf16),
            pltpu.VMEM((C, H, n), f32),
            pltpu.VMEM((C, H, n), f32),
            pltpu.VMEM((R * C, 1, 128), f32),
            dma((R,)), dma((R,)), dma((C,)), dma((C,)),
            dma((C,)), dma((C,)), dma((R * C,)), dma((R * C,)),
        ],
        compiler_params=pltpu.CompilerParams(
            collective_id=0, has_side_effects=True, vmem_limit_bytes=32 * 1024 * 1024),
    )(descriptors, lengthscale.reshape(1, D), noise.reshape(1, H), direction, residual, solution)


def solution(mesh):
    spread = P(None, ("groups", "row", "col"))
    return jax.shard_map(
        functools.partial(shards, mesh.shape["row"], mesh.shape["col"]),
        mesh=mesh,
        in_specs=(spread, P("groups"), P("groups"), spread, spread, spread),
        out_specs=(spread, spread),
        check_vma=False,
    )
```

time: 158 us -> 23.9 us (0.15)
  blocking collectives: 70.8 us -> 0 us
  waiting for transfers between devices: 40.2 us -> 0 us
  Pallas kernels: 0 us -> 18 us
  matrix products: 17.7 us -> 0 us
  between operations: 14.1 us -> 0.66 us
  local copies, waits for them, and re-layouts: 11.7 us -> 4.78 us
  other arithmetic: 2.49 us -> 0 us
    reduce_scatter x2 -> x0, waiting for transfers between devices: 39.5 us -> none  [the longest x1 20.2 us: shards(): product = lax.psum_scatter(row_acc, 'col', scatter_dimension=1, tiled=True)]
    all_gather x4 -> x0, blocking collectives: 39 us -> none  [the longest x1 14 us: shards(): lax.all_gather(direction, 'row', axis=1, tiled=True)]
    psum x1 -> x0, blocking collectives: 31.8 us -> none  [shards(): resid_sq, curvature = lax.psum((local_sq, local_curve), ('row', 'col'))]
    pallas_call x0 -> x1, Pallas kernels: none -> 18 us  [shards(): pl.pallas_call(functools.partial(kernel, R, C), out_shape=(jax.ShapeDtype...]
    dot_general x16 -> x0, matrix products: 17.7 us -> none  [the longest x4 7.22 us: per_block(): weighted = jnp.einsum('mij,mr->rij', kernel, onehot, precision=highest)]
    gather x12 -> x0, local copies, waits for them, and re-layouts: 6.68 us -> none  [the longest x4 2.25 us: per_block(): right_sq = jnp.take(column_sq, picked, axis=0)]
    unnamed x20 -> x14, local copies, waits for them, and re-layouts: 1.95 us -> 4.78 us
    mul x8 -> x0, local copies, waits for them, and re-layouts: 1.63 us -> none  [per_block(): kernel = kernel * keep[:, None, None]]
  transfers between devices with their start and end apart: 2 -> 0, of which waited for: 2 -> 0; matrix products, arithmetic and copies ran while one was open for 0% -> 0% of each run, Pallas kernels for 0% -> 0%
where the time goes in v1:
time: 23.9 us; the launch traced here: 23.4 us
  Pallas kernels  18 us (75%)
  local copies, waits for them, and re-layouts  4.78 us (20%)
  between operations  0.66 us (3%)
    pallas_call x1, Pallas kernels, shards(): pl.pallas_call(functools.partial(kernel, R, C), out_shape=(jax.ShapeDtype...  18 us
    unnamed x14, local copies, waits for them, and re-layouts  4.78 us

profile of v1, /device:TPU:0, one launch (start us, length us, event | category | flops | bytes accessed | tf_op | source)
XLA Modules:
  0.0 23.4 jit_solution(3339560600494907757)
XLA Ops:
  0.6 0.0 copy-start.4
  0.6 0.0 copy-start.5
  0.7 0.6 %copy-done.4 = f32[32]{0:T(128)S(1)} copy-done((f32[32]{0:T(128)S(1)}, f32[32]{0:T(128)}, u32[]{:S(2)}) %copy-start.4) | copy-done | bytes 152
  1.3 0.0 copy-done.5
  1.3 0.0 copy-start
  1.3 0.8 %copy-done = f32[32,256]{1,0:T(8,128)S(1)} copy-done((f32[32,256]{1,0:T(8,128)S(1)}, f32[32,256]{1,0:T(8,128)}, u32[]{:S(2)}) %copy-start) | copy-done | bytes 32792
  2.1 0.0 copy-start.1
  2.1 0.7 %copy-done.1 = f32[16,256]{1,0:T(8,128)S(1)} copy-done((f32[16,256]{1,0:T(8,128)S(1)}, f32[16,256]{1,0:T(8,128)}, u32[]{:S(2)}) %copy-start.1) | copy-done | bytes 16408
  2.8 0.0 copy-start.2
  2.8 0.7 %copy-done.2 = f32[16,256]{1,0:T(8,128)S(1)} copy-done((f32[16,256]{1,0:T(8,128)S(1)}, f32[16,256]{1,0:T(8,128)}, u32[]{:S(2)}) %copy-start.2) | copy-done | bytes 16408
  3.5 0.0 copy-start.3
  3.5 0.7 %copy-done.3 = f32[16,256]{1,0:T(8,128)S(1)} copy-done((f32[16,256]{1,0:T(8,128)S(1)}, f32[16,256]{1,0:T(8,128)}, u32[]{:S(2)}) %copy-start.3) | copy-done | bytes 16408
  4.2 18.0 %shard_map.77 = (f32[16,256]{1,0:T(8,128)S(1)}, f32[16,256]{1,0:T(8,128)S(1)}) custom-call(f32[32,256]{1,0:T(8,128)S(1)} %copy-done, f32[1,32]{1,0:T(1,128)S(1)} %bitcast.2, f32[1,16]{1,0:T(1,128)S(1)} %bitcast.3, f32[16,256]{1,0:T(8,128)S(1)} %copy-done.1, f32[16,256]{1,0:T(8,128)S(1)} %copy-done.2, f32[16,256]{1,0:T(8,128)S(1)} %copy-done.3), custom_call_target="tpu_custom_call" | custom-call | tf_op jit(solution)/shard_map/pallas_call | solution.py:171
  22.2 0.6 %copy.10 = f32[16,256]{1,0:T(8,128)} copy(f32[16,256]{1,0:T(8,128)S(1)} %get-tuple-element.4) | data formatting | bytes 32768
  22.8 0.6 %copy.11 = f32[16,256]{1,0:T(8,128)} copy(f32[16,256]{1,0:T(8,128)S(1)} %get-tuple-element.5) | data formatting | bytes 32768
Async XLA Ops:
  0.6 0.7 %copy-start.4 = (f32[32]{0:T(128)S(1)}, f32[32]{0:T(128)}, u32[]{:S(2)}) copy-start(f32[32]{0:T(128)} %param.7) | copy-start | bytes 388
  0.6 0.7 %copy-start.5 = (f32[16]{0:T(128)S(1)}, f32[16]{0:T(128)}, u32[]{:S(2)}) copy-start(f32[16]{0:T(128)} %param.8) | copy-start | bytes 196
  1.3 0.8 %copy-start = (f32[32,256]{1,0:T(8,128)S(1)}, f32[32,256]{1,0:T(8,128)}, u32[]{:S(2)}) copy-start(f32[32,256]{1,0:T(8,128)} %x_ref.1) | copy-start | bytes 98308
  2.1 0.7 %copy-start.1 = (f32[16,256]{1,0:T(8,128)S(1)}, f32[16,256]{1,0:T(8,128)}, u32[]{:S(2)}) copy-start(f32[16,256]{1,0:T(8,128)} %p_ref.1) | copy-start | bytes 49156
  2.8 0.7 %copy-start.2 = (f32[16,256]{1,0:T(8,128)S(1)}, f32[16,256]{1,0:T(8,128)}, u32[]{:S(2)}) copy-start(f32[16,256]{1,0:T(8,128)} %r_ref.1) | copy-start | bytes 49156
  3.5 0.7 %copy-start.3 = (f32[16,256]{1,0:T(8,128)S(1)}, f32[16,256]{1,0:T(8,128)}, u32[]{:S(2)}) copy-start(f32[16,256]{1,0:T(8,128)} %s_ref.1) | copy-start | bytes 49156

commit v2 on v1

v2 whole, which is shorter than its diff:
```python
import functools
import math

import jax
import jax.numpy as jnp
from jax import lax
from jax.experimental import pallas as pl
from jax.experimental.pallas import tpu as pltpu
from jax.sharding import PartitionSpec as P

MESH = pl.DeviceIdType.MESH
LOG2E = math.log2(math.e)
f32 = jnp.float32
bf16 = jnp.bfloat16


def split3(v):
    h = v.astype(bf16)
    rest = v - h.astype(f32)
    m = rest.astype(bf16)
    low = (rest - m.astype(f32)).astype(bf16)
    return h, m, low


def to_column(row, height):
    n = row.shape[1]
    wide = jnp.broadcast_to(row, (height, n))
    r = lax.broadcasted_iota(jnp.int32, (height, n), 0)
    c = lax.broadcasted_iota(jnp.int32, (height, n), 1)
    return jnp.sum(jnp.where(r == c, wide, 0.0), axis=1, keepdims=True)


def to_row(column, offset):
    h = column.shape[0]
    r = lax.broadcasted_iota(jnp.int32, (h, 128), 0)
    c = lax.broadcasted_iota(jnp.int32, (h, 128), 1)
    wide = jnp.broadcast_to(column, (h, 128))
    return jnp.sum(jnp.where(r + offset == c, wide, 0.0), axis=0, keepdims=True)


def half_square(x, xs):
    return -0.5 * jnp.sum(x * xs, axis=0, keepdims=True)


def square_rows(q, first):
    h, m, low = split3(q)
    n = q.shape[1]
    r = lax.broadcasted_iota(jnp.int32, (16, n), 0)
    base = 0 if first else 3
    other = (r >= 3 - base) & (r < 6 - base)
    out = jnp.where(other, 1.0, 0.0)
    for k, part in enumerate((h, m, low)):
        out = jnp.where(r == base + k, jnp.broadcast_to(part.astype(f32), (16, n)), out)
    return out.astype(bf16)


def stack_i(x):
    xs = x * LOG2E
    h, m, low = split3(xs)
    q = half_square(x, xs)
    pad = jnp.zeros((48, x.shape[1]), bf16)
    return jnp.concatenate([h, h, m, h, m, low, square_rows(q, True), pad], axis=0)


def stack_j(x):
    h, m, low = split3(x)
    q = half_square(x, x * LOG2E)
    pad = jnp.zeros((48, x.shape[1]), bf16)
    return jnp.concatenate([h, m, h, low, m, h, square_rows(q, False), pad], axis=0)


def kernel(R, C, x_hbm, l_hbm, n_hbm, p_hbm, r_hbm, alpha_ref, image_ref,
           xbuf, lbuf, nbuf, rbuf, jbuf, ibuf, ist, wbuf, back, backin, curve, part, rsbuf, stat,
           insem, bsend, brecv, jsend, jrecv, isend, irecv, psend, precv, ssend, srecv):
    D, n = x_hbm.shape
    H = p_hbm.shape[0]
    my_row = lax.axis_index("row")
    my_col = lax.axis_index("col")

    def peer(dr, dc):
        return {"row": lax.rem(my_row + dr, R), "col": lax.rem(my_col + dc, C)}

    half = R // 2
    upper = my_row // half
    takes_far = lax.rem(my_row + upper * (half + 1), 2) == 0
    others = [(dr, dc) for dr in range(R) for dc in range(C) if dr or dc]
    met = [(dr, 0) for dr in range(1, R)] + [(0, dc) for dc in range(1, C)]
    pairs = ((x_hbm, xbuf), (l_hbm, lbuf), (p_hbm, jbuf.at[0, D:]), (n_hbm, nbuf), (r_hbm, rbuf))
    loads = [pltpu.make_async_copy(src, dst, insem.at[k]) for k, (src, dst) in enumerate(pairs)]
    for load in loads:
        load.start()
    barrier = pltpu.get_barrier_semaphore()
    for dr, dc in met:
        pl.semaphore_signal(barrier, inc=1, device_id=peer(dr, dc), device_id_type=MESH)

    for load in loads[:3]:
        load.wait()
    jbuf[0, :D] = xbuf[...] / to_column(lbuf[...], D)

    pl.semaphore_wait(barrier, len(met))

    copies = []

    def describe(src, dst, send, recv, device):
        return pltpu.make_async_remote_copy(
            src_ref=src, dst_ref=dst, send_sem=send, recv_sem=recv,
            device_id=device, device_id_type=MESH)

    def remote(*spec):
        copy = describe(*spec)
        copy.start()
        copies.append(copy)
        return copy

    icopy, pcopy, scopy = {}, {}, {}
    jcopy = {d: describe(jbuf.at[0], jbuf.at[d], jsend.at[d], jrecv.at[d], peer(R - d, 0)) for d in range(1, half + 1)}
    bcopy = {d: describe(back.at[d], backin.at[d], bsend.at[d], brecv.at[d], peer(d, 0)) for d in range(1, half + 1)}
    for d in range(1, C):
        icopy[C - d] = remote(jbuf.at[0], ibuf.at[C - d], isend.at[C - d], irecv.at[C - d], peer(0, d))
    for d in range(1, half):
        jcopy[d].start()

    @pl.when(jnp.logical_not(takes_far))
    def _():
        jcopy[half].start()

    for load in loads[3:]:
        load.wait()
    noise = to_column(nbuf[...], H)
    resid = rbuf[...]
    resid_row = to_row(jnp.sum(resid * resid, axis=1, keepdims=True), H)
    mine = jbuf[0, D:]

    def tile(left, weights, s):
        expo = lax.dot_general(left, ist[s], (((0,), (0,)), ((), ())), preferred_element_type=f32)
        k = jnp.exp2(expo)
        k1 = k.astype(bf16)
        k2 = (k - k1.astype(f32)).astype(bf16)
        got = jnp.dot(weights, k1, preferred_element_type=f32) + jnp.dot(weights, k2, preferred_element_type=f32)
        return k1, k2, got[:H] + (got[H:2 * H] + got[2 * H:])

    left = stack_j(jbuf[0, :D])
    weights = jnp.concatenate(split3(mine), axis=0)
    wbuf[0] = weights
    for s in range(C):
        if s:
            icopy[s].wait_recv()
            ist[s] = stack_i(ibuf[s, :D])
            wbuf[s] = jnp.concatenate(split3(ibuf[s, D:]), axis=0)
        else:
            ist[s] = stack_i(jbuf[0, :D])
        part[s] = tile(left, weights, s)[2]

    curve[...] = noise * mine * mine

    def pair(d):
        jcopy[d].wait_recv()
        left = stack_j(jbuf[d, :D])
        weights = jnp.concatenate(split3(jbuf[d, D:]), axis=0)
        total = jnp.zeros((3 * H, n), f32)
        across = (((1,), (1,)), ((), ()))
        for s in range(C):
            k1, k2, got = tile(left, weights, s)
            part[s] += got
            total = total + lax.dot_general(wbuf[s], k1, across, preferred_element_type=f32)
            total = total + lax.dot_general(wbuf[s], k2, across, preferred_element_type=f32)
        total = total[:H] + (total[H:2 * H] + total[2 * H:])
        back[d] = total
        bcopy[d].start()
        curve[...] += jbuf[d, D:] * total

    for d in range(1, half):
        pair(d)

    @pl.when(takes_far)
    def _():
        pair(half)

    summed = curve[...] + mine * part[0]
    for s in range(1, C):
        pcopy[C - s] = remote(part.at[s], rsbuf.at[C - s], psend.at[C - s], precv.at[C - s], peer(0, s))
        summed = summed + ibuf[s, D:] * part[s]

    stat[0] = to_row(jnp.sum(summed, axis=1, keepdims=True), 0) + resid_row
    for dr, dc in others:
        slot = ((R - dr) % R) * C + (C - dc) % C
        scopy[slot] = remote(stat.at[0], stat.at[slot], ssend.at[slot], srecv.at[slot], peer(dr, dc))

    image = part[0] + noise * mine
    for s in range(1, C):
        pcopy[s].wait_recv()
        image = image + rsbuf[s]
    for d in range(1, half):
        bcopy[d].wait_recv()
        image = image + backin[d]
    alpha_ref[...] = jnp.zeros((H, n), f32)

    @pl.when(jnp.logical_not(takes_far))
    def _():
        bcopy[half].wait_recv()
        alpha_ref[...] = backin[half]

    image = image + alpha_ref[...]
    total = stat[0]
    for slot in range(1, R * C):
        scopy[slot].wait_recv()
        total = total + stat[slot]
    curvature = to_column(total, H)
    lane = lax.broadcasted_iota(jnp.int32, (H, 128), 1)
    sub = lax.broadcasted_iota(jnp.int32, (H, 128), 0)
    resid_sq = jnp.sum(jnp.where(lane == sub + H, jnp.broadcast_to(total, (H, 128)), 0.0), axis=1, keepdims=True)
    alpha = resid_sq / curvature
    alpha_ref[...] = jnp.broadcast_to(alpha, (H, n))
    image_ref[...] = image
    for copy in copies:
        copy.wait_send()
    for d in range(1, half):
        jcopy[d].wait_send()
        bcopy[d].wait_send()

    @pl.when(takes_far)
    def _():
        bcopy[half].wait_send()

    @pl.when(jnp.logical_not(takes_far))
    def _():
        jcopy[half].wait_send()


def shards(R, C, descriptors, lengthscale, noise, direction, residual, solution):
    D, n = descriptors.shape
    H = direction.shape[0]
    vmem = pl.BlockSpec(memory_space=pltpu.VMEM)
    dma = pltpu.SemaphoreType.DMA
    alpha, image = pl.pallas_call(
        functools.partial(kernel, R, C),
        out_shape=(jax.ShapeDtypeStruct((H, n), f32), jax.ShapeDtypeStruct((H, n), f32)),
        in_specs=[pl.BlockSpec(memory_space=pl.ANY)] * 5,
        out_specs=(vmem, vmem),
        scratch_shapes=[
            pltpu.VMEM((D, n), f32), pltpu.VMEM((1, D), f32), pltpu.VMEM((1, H), f32),
            pltpu.VMEM((H, n), f32),
            pltpu.VMEM((R, D + H, n), f32),
            pltpu.VMEM((C, D + H, n), f32),
            pltpu.VMEM((C, 256, n), bf16), pltpu.VMEM((C, 3 * H, n), bf16),
            pltpu.VMEM((R, H, n), f32), pltpu.VMEM((R, H, n), f32), pltpu.VMEM((H, n), f32),
            pltpu.VMEM((C, H, n), f32),
            pltpu.VMEM((C, H, n), f32),
            pltpu.VMEM((R * C, 1, 128), f32),
            dma((5,)), dma((R,)), dma((R,)), dma((R,)), dma((R,)), dma((C,)), dma((C,)),
            dma((C,)), dma((C,)), dma((R * C,)), dma((R * C,)),
        ],
        compiler_params=pltpu.CompilerParams(
            collective_id=0, has_side_effects=True, vmem_limit_bytes=64 * 1024 * 1024),
    )(descriptors, lengthscale.reshape(1, D), noise.reshape(1, H), direction, residual)
    return solution + alpha * direction, residual - alpha * image


def solution(mesh):
    spread = P(None, ("groups", "row", "col"))
    return jax.shard_map(
        functools.partial(shards, mesh.shape["row"], mesh.shape["col"]),
        mesh=mesh,
        in_specs=(spread, P("groups"), P("groups"), spread, spread, spread),
        out_specs=(spread, spread),
        check_vma=False,
    )
```

time: 23.9 us -> 19.8 us (0.83); the launches traced: 23.4 us -> 19.6 us
  local copies, waits for them, and re-layouts: 4.78 us -> 0 us
  other arithmetic: 0 us -> 1.41 us
  Pallas kernels: 18 us -> 17.5 us
    unnamed x14 -> x0, local copies, waits for them, and re-layouts: 4.78 us -> none
    sub x0 -> x1, other arithmetic: none -> 1.41 us  [shards(): return (solution + alpha * direction, residual - alpha * image)]
    pallas_call x1, Pallas kernels: 18 us -> 17.5 us  [shards(): pl.pallas_call(functools.partial(kernel, R, C), out_shape=(jax.ShapeDtype...]
where the time goes in v2:
time: 19.8 us; the launch traced here: 19.6 us
  Pallas kernels  17.5 us (88%)
  other arithmetic  1.41 us (7%)
  between operations  0.64 us (3%)
    pallas_call x1, Pallas kernels, shards(): pl.pallas_call(functools.partial(kernel, R, C), out_shape=(jax.ShapeDtype...  17.5 us
    sub x1, other arithmetic, shards(): return (solution + alpha * direction, residual - alpha * image)  1.41 us

profile of v2, /device:TPU:0, one launch (start us, length us, event | category | flops | bytes accessed | tf_op | source)
XLA Modules:
  0.0 19.6 jit_solution(6547527889657363574)
XLA Ops:
  0.6 17.5 %shard_map.77 = (f32[16,256]{1,0:T(8,128)}, f32[16,256]{1,0:T(8,128)}) custom-call(f32[32,256]{1,0:T(8,128)} %x_hbm.1, f32[1,32]{1,0:T(1,128)} %bitcast.2, f32[1,16]{1,0:T(1,128)} %bitcast.3, f32[16,256]{1,0:T(8,128)} %p_hbm.1, f32[16,256]{1,0:T(8,128)} %r_hbm.1), custom_call_target="tpu_custom_call" | custom-call | tf_op jit(solution)/shard_map/pallas_call | solution.py:235
  18.2 1.4 %multiply_subtract_fusion = (f32[16,256]{1,0:T(8,128)}, f32[16,256]{1,0:T(8,128)}) fusion(f32[16,256]{1,0:T(8,128)} %r_hbm.1, f32[16,256]{1,0:T(8,128)} %get-tuple-element.4, f32[16,256]{1,0:T(8,128)} %get-tuple-element.5, f32[16,256]{1,0:T(8,128)} %param.11, f32[16,256]{1,0:T(8,128)} %p_hbm.1), kind=kLoop, calls=%fused_computation | loop fusion | flops 16384 | bytes 114688 | tf_op jit(solution)/shard_map/sub | solution.py:256

commit v3 on v2

--- a/solution.py
+++ b/solution.py
@@ -82,7 +82,7 @@
 
     half = R // 2
     upper = my_row // half
-    takes_far = lax.rem(my_row + upper * (half + 1), 2) == 0
+    takes_far = lax.rem(my_row + upper * (half + 1), 2) == 1
     others = [(dr, dc) for dr in range(R) for dc in range(C) if dr or dc]
     met = [(dr, 0) for dr in range(1, R)] + [(0, dc) for dc in range(1, C)]
     pairs = ((x_hbm, xbuf), (l_hbm, lbuf), (p_hbm, jbuf.at[0, D:]), (n_hbm, nbuf), (r_hbm, rbuf))
@@ -115,14 +115,15 @@
     icopy, pcopy, scopy = {}, {}, {}
     jcopy = {d: describe(jbuf.at[0], jbuf.at[d], jsend.at[d], jrecv.at[d], peer(R - d, 0)) for d in range(1, half + 1)}
     bcopy = {d: describe(back.at[d], backin.at[d], bsend.at[d], brecv.at[d], peer(d, 0)) for d in range(1, half + 1)}
+    for d in range(1, half):
+        jcopy[d].start()
+
+    @pl.when(jnp.logical_not(takes_far))
+    def _():
+        jcopy[half].start()
+
     for d in range(1, C):
         icopy[C - d] = remote(jbuf.at[0], ibuf.at[C - d], isend.at[C - d], irecv.at[C - d], peer(0, d))
-    for d in range(1, half):
-        jcopy[d].start()
-
-    @pl.when(jnp.logical_not(takes_far))
-    def _():
-        jcopy[half].start()
 
     for load in loads[3:]:
         load.wait()
@@ -132,14 +133,14 @@
     mine = jbuf[0, D:]
 
     def tile(left, weights, s):
-        expo = lax.dot_general(left, ist[s], (((0,), (0,)), ((), ())), preferred_element_type=f32)
+        expo = jnp.dot(left, ist[s], preferred_element_type=f32)
         k = jnp.exp2(expo)
         k1 = k.astype(bf16)
         k2 = (k - k1.astype(f32)).astype(bf16)
         got = jnp.dot(weights, k1, preferred_element_type=f32) + jnp.dot(weights, k2, preferred_element_type=f32)
         return k1, k2, got[:H] + (got[H:2 * H] + got[2 * H:])
 
-    left = stack_j(jbuf[0, :D])
+    left = stack_j(jbuf[0, :D]).T
     weights = jnp.concatenate(split3(mine), axis=0)
     wbuf[0] = weights
     for s in range(C):
@@ -155,7 +156,7 @@
 
     def pair(d):
         jcopy[d].wait_recv()
-        left = stack_j(jbuf[d, :D])
+        left = stack_j(jbuf[d, :D]).T
         weights = jnp.concatenate(split3(jbuf[d, D:]), axis=0)
         total = jnp.zeros((3 * H, n), f32)
         across = (((1,), (1,)), ((), ()))

time: 19.8 us -> 18.7 us (0.944)
  Pallas kernels: 17.5 us -> 16.4 us
    pallas_call x1, Pallas kernels: 17.5 us -> 16.4 us  [shards(): pl.pallas_call(functools.partial(kernel, R, C), out_shape=(jax.ShapeDtype...]
where the time goes in v3:
time: 18.7 us; the launch traced here: 18.5 us
  Pallas kernels  16.4 us (88%)
  other arithmetic  1.41 us (8%)
  between operations  0.64 us (3%)
    pallas_call x1, Pallas kernels, shards(): pl.pallas_call(functools.partial(kernel, R, C), out_shape=(jax.ShapeDtype...  16.4 us
    sub x1, other arithmetic, shards(): return (solution + alpha * direction, residual - alpha * image)  1.41 us

profile of v3, /device:TPU:0, one launch (start us, length us, event | category | flops | bytes accessed | tf_op | source)
XLA Modules:
  0.0 18.5 jit_solution(16239411037544814033)
XLA Ops:
  0.6 16.4 %shard_map.77 = (f32[16,256]{1,0:T(8,128)}, f32[16,256]{1,0:T(8,128)}) custom-call(f32[32,256]{1,0:T(8,128)} %x_hbm.1, f32[1,32]{1,0:T(1,128)} %bitcast.2, f32[1,16]{1,0:T(1,128)} %bitcast.3, f32[16,256]{1,0:T(8,128)} %p_hbm.1, f32[16,256]{1,0:T(8,128)} %r_hbm.1), custom_call_target="tpu_custom_call" | custom-call | tf_op jit(solution)/shard_map/pallas_call | solution.py:236
  17.1 1.4 %multiply_subtract_fusion = (f32[16,256]{1,0:T(8,128)}, f32[16,256]{1,0:T(8,128)}) fusion(f32[16,256]{1,0:T(8,128)} %r_hbm.1, f32[16,256]{1,0:T(8,128)} %get-tuple-element.4, f32[16,256]{1,0:T(8,128)} %get-tuple-element.5, f32[16,256]{1,0:T(8,128)} %param.11, f32[16,256]{1,0:T(8,128)} %p_hbm.1), kind=kLoop, calls=%fused_computation | loop fusion | flops 16384 | bytes 114688 | tf_op jit(solution)/shard_map/sub | solution.py:257

commit v4 on v3

--- a/solution.py
+++ b/solution.py
@@ -159,13 +159,14 @@
         left = stack_j(jbuf[d, :D]).T
         weights = jnp.concatenate(split3(jbuf[d, D:]), axis=0)
         total = jnp.zeros((3 * H, n), f32)
+        minor = jnp.zeros((2 * H, n), f32)
         across = (((1,), (1,)), ((), ()))
         for s in range(C):
             k1, k2, got = tile(left, weights, s)
             part[s] += got
             total = total + lax.dot_general(wbuf[s], k1, across, preferred_element_type=f32)
-            total = total + lax.dot_general(wbuf[s], k2, across, preferred_element_type=f32)
-        total = total[:H] + (total[H:2 * H] + total[2 * H:])
+            minor = minor + lax.dot_general(wbuf[s, :2 * H], k2, across, preferred_element_type=f32)
+        total = total[:H] + (total[H:2 * H] + total[2 * H:]) + (minor[:H] + minor[H:])
         back[d] = total
         bcopy[d].start()
         curve[...] += jbuf[d, D:] * total

time: 18.7 us -> 18.4 us (0.984)
  Pallas kernels: 16.4 us -> 16.1 us
    pallas_call x1, Pallas kernels: 16.4 us -> 16.1 us  [shards(): pl.pallas_call(functools.partial(kernel, R, C), out_shape=(jax.ShapeDtype...]
where the time goes in v4:
time: 18.4 us; the launch traced here: 18.1 us
  Pallas kernels  16.1 us (88%)
  other arithmetic  1.41 us (8%)
  between operations  0.64 us (3%)
    pallas_call x1, Pallas kernels, shards(): pl.pallas_call(functools.partial(kernel, R, C), out_shape=(jax.ShapeDtype...  16.1 us
    sub x1, other arithmetic, shards(): return (solution + alpha * direction, residual - alpha * image)  1.41 us

profile of v4, /device:TPU:0, one launch (start us, length us, event | category | flops | bytes accessed | tf_op | source)
XLA Modules:
  0.0 18.1 jit_solution(6637783808137617503)
XLA Ops:
  0.6 16.1 %shard_map.77 = (f32[16,256]{1,0:T(8,128)}, f32[16,256]{1,0:T(8,128)}) custom-call(f32[32,256]{1,0:T(8,128)} %x_hbm.1, f32[1,32]{1,0:T(1,128)} %bitcast.2, f32[1,16]{1,0:T(1,128)} %bitcast.3, f32[16,256]{1,0:T(8,128)} %p_hbm.1, f32[16,256]{1,0:T(8,128)} %r_hbm.1), custom_call_target="tpu_custom_call" | custom-call | tf_op jit(solution)/shard_map/pallas_call | solution.py:237
  16.7 1.4 %multiply_subtract_fusion = (f32[16,256]{1,0:T(8,128)}, f32[16,256]{1,0:T(8,128)}) fusion(f32[16,256]{1,0:T(8,128)} %r_hbm.1, f32[16,256]{1,0:T(8,128)} %get-tuple-element.4, f32[16,256]{1,0:T(8,128)} %get-tuple-element.5, f32[16,256]{1,0:T(8,128)} %param.11, f32[16,256]{1,0:T(8,128)} %p_hbm.1), kind=kLoop, calls=%fused_computation | loop fusion | flops 16384 | bytes 114688 | tf_op jit(solution)/shard_map/sub | solution.py:258

commit v5 on v4

--- a/solution.py
+++ b/solution.py
@@ -87,12 +87,14 @@
     met = [(dr, 0) for dr in range(1, R)] + [(0, dc) for dc in range(1, C)]
     pairs = ((x_hbm, xbuf), (l_hbm, lbuf), (p_hbm, jbuf.at[0, D:]), (n_hbm, nbuf), (r_hbm, rbuf))
     loads = [pltpu.make_async_copy(src, dst, insem.at[k]) for k, (src, dst) in enumerate(pairs)]
-    for load in loads:
+    for load in loads[:3]:
         load.start()
     barrier = pltpu.get_barrier_semaphore()
     for dr, dc in met:
         pl.semaphore_signal(barrier, inc=1, device_id=peer(dr, dc), device_id_type=MESH)
 
+    for load in loads[3:]:
+        load.start()
     for load in loads[:3]:
         load.wait()
     jbuf[0, :D] = xbuf[...] / to_column(lbuf[...], D)
@@ -180,13 +182,15 @@
 
     summed = curve[...] + mine * part[0]
     for s in range(1, C):
-        pcopy[C - s] = remote(part.at[s], rsbuf.at[C - s], psend.at[C - s], precv.at[C - s], peer(0, s))
         summed = summed + ibuf[s, D:] * part[s]
 
     stat[0] = to_row(jnp.sum(summed, axis=1, keepdims=True), 0) + resid_row
-    for dr, dc in others:
+    for dr, dc in reversed(others):
         slot = ((R - dr) % R) * C + (C - dc) % C
         scopy[slot] = remote(stat.at[0], stat.at[slot], ssend.at[slot], srecv.at[slot], peer(dr, dc))
+
+    for s in range(1, C):
+        pcopy[C - s] = remote(part.at[s], rsbuf.at[C - s], psend.at[C - s], precv.at[C - s], peer(0, s))
 
     image = part[0] + noise * mine
     for s in range(1, C):

time: 18.4 us -> 18.4 us (level)
  no operation moved by 1% of the time
where the time goes in v5:
time: 18.4 us; the launch traced here: 18.1 us
  Pallas kernels  16.1 us (88%)
  other arithmetic  1.41 us (8%)
  between operations  0.64 us (3%)
    pallas_call x1, Pallas kernels, shards(): pl.pallas_call(functools.partial(kernel, R, C), out_shape=(jax.ShapeDtype...  16.1 us
    sub x1, other arithmetic, shards(): return (solution + alpha * direction, residual - alpha * image)  1.41 us

profile of v5, /device:TPU:0, one launch (start us, length us, event | category | flops | bytes accessed | tf_op | source)
XLA Modules:
  0.0 18.1 jit_solution(8369448668795657999)
XLA Ops:
  0.6 16.1 %shard_map.77 = (f32[16,256]{1,0:T(8,128)}, f32[16,256]{1,0:T(8,128)}) custom-call(f32[32,256]{1,0:T(8,128)} %x_hbm.1, f32[1,32]{1,0:T(1,128)} %bitcast.2, f32[1,16]{1,0:T(1,128)} %bitcast.3, f32[16,256]{1,0:T(8,128)} %p_hbm.1, f32[16,256]{1,0:T(8,128)} %r_hbm.1), custom_call_target="tpu_custom_call" | custom-call | tf_op jit(solution)/shard_map/pallas_call | solution.py:241
  16.7 1.4 %multiply_subtract_fusion = (f32[16,256]{1,0:T(8,128)}, f32[16,256]{1,0:T(8,128)}) fusion(f32[16,256]{1,0:T(8,128)} %r_hbm.1, f32[16,256]{1,0:T(8,128)} %get-tuple-element.4, f32[16,256]{1,0:T(8,128)} %get-tuple-element.5, f32[16,256]{1,0:T(8,128)} %param.11, f32[16,256]{1,0:T(8,128)} %p_hbm.1), kind=kLoop, calls=%fused_computation | loop fusion | flops 16384 | bytes 114688 | tf_op jit(solution)/shard_map/sub | solution.py:262
